TPU v7x, 256 devices: a whole 4x4x8 slice. The times are simulated.
256 devices in a mesh: seq: 16 (over z, core), head: 4 (over x), dp: 4 (over y).
Axes of the slice: x: 4, y: 4, z: 8, core: 2. Of those that a mesh axis runs over, the one named last changes fastest.
Arguments:
- self_queries: bfloat16 [4, 2048, 2560], P('dp', ('seq', 'head')), may hold values from -8 to 8
- self_keys: bfloat16 [4, 2048, 2560], P('dp', ('seq', 'head')), may hold values from -4 to 4
- self_values: bfloat16 [4, 2048, 2560], P('dp', ('seq', 'head')), may hold values from -6 to 6
- self_cotangent: bfloat16 [4, 2048, 2560], P('dp', ('seq', 'head')), may hold values from -6 to 6
- text_queries: bfloat16 [4, 4096, 2560], P('dp', 'seq', 'head'), may hold values from -8 to 8
- memory_keys: bfloat16 [4, 2048, 2560], P('dp', 'seq', 'head'), may hold values from -4 to 4
- memory_values: bfloat16 [4, 2048, 2560], P('dp', 'seq', 'head'), may hold values from -6 to 6
- text_cotangent: bfloat16 [4, 4096, 2560], P('dp', 'seq', 'head'), may hold values from -6 to 6
- slopes: float32 [2, 20], P(None, 'head'), may hold values from 0.01 to 0.3
- page_counts: int32 [4, 4], P('dp'), may hold values from 1 to 1024, as said below
- page_cols: int32 [4, 4], P('dp'), may hold values from 4 to 64
- text_page: int32 [4, 4096], P('dp'), may hold values from 0 to 3, as said below
Outputs:
- self_query_grad: bfloat16 [4, 2048, 2560], P('dp', ('seq', 'head'))
- self_key_grad: bfloat16 [4, 2048, 2560], P('dp', ('seq', 'head'))
- self_value_grad: bfloat16 [4, 2048, 2560], P('dp', ('seq', 'head'))
- slope_grad: float32 [2, 20], P(None, 'head')
- text_query_grad: bfloat16 [4, 4096, 2560], P('dp', 'seq', 'head')
- memory_key_grad: bfloat16 [4, 2048, 2560], P('dp', 'seq', 'head')
- memory_value_grad: bfloat16 [4, 2048, 2560], P('dp', 'seq', 'head')
Inputs may be any that keep to these rules, and one draw needn't show every extreme that they name: `page_counts`: each pack's counts sum to 2048; one page of every pack has exactly 1024 patches. `text_page`: never falls along a pack's text rows; every page has at least one text row.
All inputs are finite; a program needn't handle non-finite values.
Results may differ from a plain program's by a relative error of at most 0.006.
Values may be sent and summed in bfloat16 or wider, within the bound.
No kernel may reach another device: no remote copies, remote signals or barrier semaphores. Data moves between devices by JAX's collectives and lax.ppermute only.
A program may use at most 128 MiB of HBM per device.

v0:
```python
import jax
import jax.numpy as jnp
from jax import lax
from jax.sharding import PartitionSpec as P

MASK_FILL = -1e30


def page_layout(counts, widths, patch_total):
    page_ends = jnp.cumsum(counts)
    starts = page_ends - counts
    positions = jnp.arange(patch_total, dtype=jnp.int32)
    page_ids = jnp.sum((positions[:, None] >= page_ends[None, :]).astype(jnp.int32), axis=1)
    one_hot = page_ids[:, None] == jnp.arange(counts.shape[0], dtype=jnp.int32)[None, :]
    page_start = jnp.sum(jnp.where(one_hot, starts[None, :], 0), axis=1)
    page_width = jnp.sum(jnp.where(one_hot, widths[None, :], 0), axis=1)
    offsets = positions - page_start
    return (page_ids, offsets // page_width, offsets % page_width)


def take_rows(vector, row_start, row_count):
    return lax.dynamic_slice_in_dim(vector, row_start, row_count, 0)


def heads_of(matrix, head_count):
    return matrix.reshape(matrix.shape[0], head_count, -1)


def alibi(slopes, query_layout, key_layout):
    row_gap = jnp.abs(query_layout[1][:, None] - key_layout[1][None, :]).astype(jnp.float32)
    col_gap = jnp.abs(query_layout[2][:, None] - key_layout[2][None, :]).astype(jnp.float32)
    same_page = query_layout[0][:, None] == key_layout[0][None, :]
    decay = -(slopes[0][:, None, None] * row_gap[None] + slopes[1][:, None, None] * col_gap[None])
    return (jnp.where(same_page[None], decay, MASK_FILL), row_gap, col_gap)


def query_side(queries, key_rows, value_rows, grad_rows, logit_bias):
    inv_root = queries.shape[2] ** (-0.5)
    scores = (
        jnp.einsum("rhs,khs->hrk", queries, key_rows, preferred_element_type=jnp.float32) * inv_root
        + logit_bias
    )
    row_max = jnp.max(scores, axis=2, keepdims=True)
    weights = jnp.exp(scores - row_max)
    row_total = jnp.sum(weights, axis=2, keepdims=True)
    softmax_w = weights / row_total
    log_total = (row_max + jnp.log(row_total))[:, :, 0]
    grad_probs = jnp.einsum(
        "rhs,khs->hrk", grad_rows, value_rows, preferred_element_type=jnp.float32
    )
    row_delta = jnp.sum(softmax_w * grad_probs, axis=2, keepdims=True)
    grad_scores = softmax_w * (grad_probs - row_delta)
    grad_scores_b = grad_scores.astype(jnp.bfloat16)
    query_grad = (
        jnp.einsum("hrk,khs->rhs", grad_scores_b, key_rows, preferred_element_type=jnp.float32)
        * inv_root
    )
    return (
        query_grad,
        grad_scores,
        grad_scores_b,
        softmax_w.astype(jnp.bfloat16),
        log_total,
        row_delta[:, :, 0],
    )


def key_terms(grad_scores_b, softmax_b, queries, grad_rows, row_count):
    inv_root = queries.shape[3] ** (-0.5)
    key_grad = (
        jnp.einsum("chrk,crhs->khs", grad_scores_b, queries, preferred_element_type=jnp.float32)
        * inv_root
    )
    value_grad = jnp.einsum(
        "chrk,crhs->khs", softmax_b, grad_rows, preferred_element_type=jnp.float32
    )
    return jnp.stack([key_grad.reshape(row_count, -1), value_grad.reshape(row_count, -1)], axis=1)


def local(
    self_queries,
    self_keys,
    self_values,
    self_cotangent,
    text_queries,
    memory_keys,
    memory_values,
    text_cotangent,
    slopes,
    page_counts,
    page_cols,
    text_page,
):
    head_count = slopes.shape[1]
    regrouped = (
        lax.all_to_all(self_queries[0], "head", split_axis=1, concat_axis=0, tiled=True),
        lax.all_to_all(self_keys[0], "head", split_axis=1, concat_axis=0, tiled=True),
        lax.all_to_all(self_values[0], "head", split_axis=1, concat_axis=0, tiled=True),
        lax.all_to_all(self_cotangent[0], "head", split_axis=1, concat_axis=0, tiled=True),
    )
    local_queries, local_keys, local_values, local_grads = regrouped
    patch_rows = local_queries.shape[0]
    all_keys, all_values = (
        lax.all_gather(local_keys, "seq", axis=0, tiled=True),
        lax.all_gather(local_values, "seq", axis=0, tiled=True),
    )
    patch_total = all_keys.shape[0]
    whole_layout = page_layout(page_counts[0], page_cols[0], patch_total)
    own_start = lax.axis_index("seq") * patch_rows
    own_layout = tuple((take_rows(item, own_start, patch_rows) for item in whole_layout))
    self_bias, row_gap, col_gap = alibi(slopes, own_layout, whole_layout)
    query_heads = heads_of(local_queries, head_count)
    grad_heads = heads_of(local_grads, head_count)
    self_dq, self_ds, self_ds_b, self_p_b, self_lse, self_delta = query_side(
        query_heads,
        heads_of(all_keys, head_count),
        heads_of(all_values, head_count),
        grad_heads,
        self_bias,
    )
    slope_local = -jnp.stack(
        [
            jnp.sum(self_ds * row_gap[None], axis=(1, 2)),
            jnp.sum(self_ds * col_gap[None], axis=(1, 2)),
        ]
    )
    self_ds_blocks = self_ds_b[None]
    self_p_blocks = self_p_b[None]
    query_blocks = query_heads[None]
    grad_blocks = grad_heads[None]
    self_pair = lax.psum_scatter(
        key_terms(
            self_ds_blocks,
            self_p_blocks,
            query_blocks,
            grad_blocks,
            patch_rows * lax.axis_size("seq"),
        ),
        "seq",
        scatter_dimension=0,
        tiled=True,
    )
    self_dk = self_pair[:, 0]
    self_dv = self_pair[:, 1]
    restored = (
        lax.all_to_all(
            self_dq.reshape(patch_rows, -1).astype(jnp.bfloat16),
            "head",
            split_axis=0,
            concat_axis=1,
            tiled=True,
        ),
        lax.all_to_all(
            self_dk.astype(jnp.bfloat16), "head", split_axis=0, concat_axis=1, tiled=True
        ),
        lax.all_to_all(
            self_dv.astype(jnp.bfloat16), "head", split_axis=0, concat_axis=1, tiled=True
        ),
    )
    slope_grad = lax.psum(slope_local, ("seq", "dp")) / patch_total
    memory_all_keys, memory_all_values = (
        lax.all_gather(memory_keys[0], "seq", axis=0, tiled=True),
        lax.all_gather(memory_values[0], "seq", axis=0, tiled=True),
    )
    memory_all_key_heads = heads_of(memory_all_keys, head_count)
    memory_all_value_heads = heads_of(memory_all_values, head_count)
    text_rows = text_queries.shape[1]
    text_start = lax.axis_index("seq") * text_rows
    text_ids = text_page[0]
    own_text = take_rows(text_ids, text_start, text_rows)
    text_query_heads = heads_of(text_queries[0], head_count)
    text_grad_heads = heads_of(text_cotangent[0], head_count)
    block_count = text_rows // text_rows
    text_query_blocks = text_query_heads.reshape(block_count, text_rows, head_count, -1)
    text_grad_blocks = text_grad_heads.reshape(block_count, text_rows, head_count, -1)

    def cross_block(inputs):
        block_queries, block_grads, block_pages = inputs
        block_bias = jnp.where(
            block_pages[:, None] == whole_layout[0][None, :], 0.0, MASK_FILL
        ).astype(jnp.float32)[None]
        result = query_side(
            block_queries, memory_all_key_heads, memory_all_value_heads, block_grads, block_bias
        )
        return (result[0], result[2], result[3], result[4], result[5])

    cross_out = lax.map(
        cross_block, (text_query_blocks, text_grad_blocks, own_text.reshape(block_count, text_rows))
    )
    text_dq = cross_out[0].reshape(text_rows, -1)
    text_ds_b = cross_out[1]
    text_p_b = cross_out[2]
    memory_pair = lax.psum_scatter(
        key_terms(
            text_ds_b,
            text_p_b,
            text_query_blocks,
            text_grad_blocks,
            patch_rows * lax.axis_size("seq"),
        ),
        "seq",
        scatter_dimension=0,
        tiled=True,
    )
    memory_dk = memory_pair[:, 0]
    memory_dv = memory_pair[:, 1]
    return (
        restored[0][None],
        restored[1][None],
        restored[2][None],
        slope_grad,
        text_dq.astype(jnp.bfloat16)[None],
        memory_dk.astype(jnp.bfloat16)[None],
        memory_dv.astype(jnp.bfloat16)[None],
    )


def solution(mesh):
    in_specs = (
        P("dp", ("seq", "head"), None),
        P("dp", ("seq", "head"), None),
        P("dp", ("seq", "head"), None),
        P("dp", ("seq", "head"), None),
        P("dp", "seq", "head"),
        P("dp", "seq", "head"),
        P("dp", "seq", "head"),
        P("dp", "seq", "head"),
        P(None, "head"),
        P("dp", None),
        P("dp", None),
        P("dp", None),
    )
    out_specs = (
        P("dp", ("seq", "head"), None),
        P("dp", ("seq", "head"), None),
        P("dp", ("seq", "head"), None),
        P(None, "head"),
        P("dp", "seq", "head"),
        P("dp", "seq", "head"),
        P("dp", "seq", "head"),
    )
    return jax.shard_map(local, mesh=mesh, in_specs=in_specs, out_specs=out_specs, check_vma=False)
```

profile of v0, /device:TPU:2, one launch (start us, length us, event | category | flops | bytes accessed | tf_op | source)
XLA Modules:
  0.0 406.0 jit_solution(9305916653580052399)
XLA Ops:
  7.3 1.0 all_to_all.85
  8.3 10.0 %all_to_all.109 = bf16[32,4,640]{2,0,1:T(8,128)(2,1)} all-to-all(bf16[32,4,640]{2,0,1:T(8,128)(2,1)S(1)} %copy.117), channel_id=1, replica_groups=mesh['seq'=16,'head'=4,'dp'=4] {'head'}, dimensions={1} | all-to-all | bytes 327680 | tf_op jit(solution)/shard_map/all_to_all | solution.py:97
  18.4 1.0 all_to_all.92
  19.4 9.2 %all_to_all.110 = bf16[32,4,640]{2,0,1:T(8,128)(2,1)} all-to-all(bf16[32,4,640]{2,0,1:T(8,128)(2,1)S(1)} %copy.122), channel_id=1, replica_groups=mesh['seq'=16,'head'=4,'dp'=4] {'head'}, dimensions={1} | all-to-all | bytes 327680 | tf_op jit(solution)/shard_map/all_to_all | solution.py:98
  28.6 1.7 copy.136
  30.4 1.0 all_to_all.82
  31.4 0.7 copy.116
  32.1 4.7 %all-to-all-start = ((bf16[32,4,640]{2,0,1:T(8,128)(2,1)}), bf16[32,4,640]{2,0,1:T(8,128)(2,1)S(1)}, u32[]{:S(2)}, u32[]{:S(2)}) async-start(bf16[32,4,640]{2,0,1:T(8,128)(2,1)} %copy.116), calls=%async_computation | async-start | bytes 327680 | tf_op jit(solution)/shard_map/all_to_all | solution.py:96
  36.8 1.7 copy.140
  38.6 0.8 reduce-window.4
  39.4 0.7 fusion.25
  40.2 0.8 select_reduce_fusion.1
  41.4 1.8 abs_convert_fusion
  43.5 0.7 copy.121
  44.2 4.8 %all-to-all-start.2 = ((bf16[32,4,640]{2,0,1:T(8,128)(2,1)}), bf16[32,4,640]{2,0,1:T(8,128)(2,1)S(1)}, u32[]{:S(2)}, u32[]{:S(2)}) async-start(bf16[32,4,640]{2,0,1:T(8,128)(2,1)} %copy.121), calls=%async_computation.2 | async-start | bytes 327680 | tf_op jit(solution)/shard_map/all_to_all | solution.py:99
  49.4 4.3 %all-to-all-done.2 = bf16[32,4,640]{2,0,1:T(8,128)(2,1)S(1)} async-done(((bf16[32,4,640]{2,0,1:T(8,128)(2,1)}), bf16[32,4,640]{2,0,1:T(8,128)(2,1)S(1)}, u32[]{:S(2)}, u32[]{:S(2)}) %all-to-all-start.2) | async-done | bytes 163872 | tf_op jit(solution)/shard_map/all_to_all | solution.py:99
  54.1 6.2 %all-gather.7.cloned.1.call-done = bf16[2048,640]{1,0:T(8,128)(2,1)} async-done(((bf16[128,640]{1,0:T(8,128)(2,1)}), bf16[2048,640]{1,0:T(8,128)(2,1)}) %all-gather.7.cloned.1.call-update) | async-done | bytes 2621456 | tf_op jit(solution)/shard_map/all_gather | solution.py:104
  60.3 3.0 copy.118
  63.3 37.8 %all-gather.9.cloned.1.call-done = bf16[2048,640]{1,0:T(8,128)(2,1)} async-done(((bf16[128,640]{1,0:T(8,128)(2,1)}), bf16[2048,640]{1,0:T(8,128)(2,1)}) %all-gather.9.cloned.1.call-update) | async-done | bytes 2621456 | tf_op jit(solution)/shard_map/all_gather | solution.py:105
  101.0 4.5 %copy.123 = bf16[2048,640]{0,1:T(8,128)(2,1)} copy(bf16[2048,640]{1,0:T(8,128)(2,1)} %all-gather.9.cloned.1.call-done) | data formatting | bytes 5242880 | tf_op jit(solution)/shard_map/all_gather | solution.py:105
  105.5 3.6 select_add_fusion
  109.1 1.6 fusion.28
  110.7 1.0 copy-done.4
  111.7 1.0 copy-done.7
  112.7 1.3 multiply_reduce_fusion.3
  114.3 2.4 multiply_reduce_fusion.2
  116.7 3.2 convolution_multiply_fusion
  119.8 6.0 %copy.131 = f32[2048,1,640]{2,0,1:T(8,128)} copy(f32[2048,1,640]{0,2,1:T(8,128)} %bitcast.79) | data formatting | bytes 10485760 | tf_op jit(solution)/shard_map/stack;reshape | solution.py:77
  125.8 8.0 %fusion.7 = f32[5,2048,128]{1,2,0:T(8,128)} fusion(bf16[128,5,128]{0,2,1:T(8,128)(2,1)S(1)} %copy.130, f32[5,128]{1,0:T(8,128)S(1)} %get-tuple-element.85, f32[5,128,2048]{2,1,0:T(8,128)} %copy-done.4), kind=kOutput, calls=%fused_computation.22 | convolution fusion | flops 339479168 | bytes 10652160 | tf_op jit(solution)/shard_map/chrk,crhs->khs/dot_general | solution.py:74
  133.7 5.9 %copy.132 = f32[2048,1,640]{2,0,1:T(8,128)} copy(f32[2048,1,640]{0,2,1:T(8,128)} %bitcast.84) | data formatting | bytes 10485760 | tf_op jit(solution)/shard_map/stack;reshape | solution.py:77
  139.6 8.8 %pad_maximum_fusion = f32[2048,2,640]{2,0,1:T(8,128)} fusion(f32[2048,1,640]{2,0,1:T(8,128)} %copy.132, f32[2048,1,640]{2,0,1:T(8,128)} %copy.131), kind=kLoop, calls=%fused_computation.2 | loop fusion | flops 2621440 | bytes 20971520 | tf_op jit(solution)/shard_map/stack | solution.py:77
  148.7 0.7 copy-done.8
  149.6 1.1 copy.139
  150.8 1.6 compare_select_fusion
  152.4 9.5 %fusion.29 = (f32[5,256]{1,0:T(8,128)S(1)}, f32[5,256,2048]{2,1,0:T(8,128)}) fusion(f32[256,2048]{1,0:T(8,128)} %compare_select_fusion, bf16[256,5,128]{0,2,1:T(8,128)(2,1)S(1)} %bitcast.87, bf16[2048,5,128]{0,2,1:T(8,128)(2,1)} %bitcast.104), kind=kOutput, calls=%fused_computation.62 | convolution fusion | flops 681576448 | bytes 15537152 | tf_op jit(solution)/shard_map/while/body/eval_jaxpr/sub | solution.py:44
  161.8 27.1 %all-gather.13.cloned.1.call-done = bf16[1,2048,640]{1,2,0:T(8,128)(2,1)} async-done(((bf16[1,128,640]{1,2,0:T(8,128)(2,1)}), bf16[1,2048,640]{1,2,0:T(8,128)(2,1)}) %all-gather.13.cloned.1.call-update) | async-done | bytes 2621456 | tf_op jit(solution)/shard_map/all_gather | solution.py:163
  189.0 6.1 %multiply_reduce_fusion = (f32[5,256]{1,0:T(8,128)S(1)}, f32[5,256,2048]{2,1,0:T(8,128)S(1)}) fusion(f32[5,256,2048]{2,1,0:T(8,128)} %get-tuple-element.90, f32[5,256]{1,0:T(8,128)S(1)} %get-tuple-element.89, bf16[256,5,128]{0,2,1:T(8,128)(2,1)S(1)} %bitcast.96, bf16[2048,5,128]{0,2,1:T(8,128)(2,1)} %bitcast.106), kind=kOutput, calls=%fused_computation.5 | convolution fusion | flops 678951680 | bytes 23930880 | tf_op jit(solution)/shard_map/while/body/eval_jaxpr/rhs,khs->hrk/dot_general | solution.py:48
  195.1 1.1 slice-done.1
  196.2 0.6 slice-done.2
  196.8 1.8 multiply_convert_fusion
  198.6 3.9 convolution_multiply_fusion.1
  202.6 5.9 %copy.143 = f32[2048,1,640]{2,0,1:T(8,128)} copy(f32[2048,1,640]{0,2,1:T(8,128)} %bitcast.78) | data formatting | bytes 10485760 | tf_op jit(solution)/shard_map/stack;reshape | solution.py:77
  208.5 7.4 %fusion.3 = f32[5,2048,128]{1,2,0:T(8,128)} fusion(bf16[256,5,128]{0,2,1:T(8,128)(2,1)S(1)} %bitcast.97, f32[5,256,2048]{2,1,0:T(8,128)} %get-tuple-element.90, f32[5,256]{1,0:T(8,128)S(1)} %get-tuple-element.89), kind=kOutput, calls=%fused_computation.9 | convolution fusion | flops 676331520 | bytes 16061440 | tf_op jit(solution)/shard_map/chrk,crhs->khs/dot_general | solution.py:74
  215.9 5.9 %copy.144 = f32[2048,1,640]{2,0,1:T(8,128)} copy(f32[2048,1,640]{0,2,1:T(8,128)} %bitcast.85) | data formatting | bytes 10485760 | tf_op jit(solution)/shard_map/stack;reshape | solution.py:77
  221.9 8.7 %pad_maximum_fusion.1 = f32[2048,2,640]{2,0,1:T(8,128)} fusion(f32[2048,1,640]{2,0,1:T(8,128)} %copy.144, f32[2048,1,640]{2,0,1:T(8,128)} %copy.143), kind=kLoop, calls=%fused_computation.3 | loop fusion | flops 2621440 | bytes 20971520 | tf_op jit(solution)/shard_map/stack | solution.py:77
  230.6 5.3 %fusion.14 = bf16[5,256,128]{1,2,0:T(8,128)(2,1)S(1)} fusion(bf16[5,256,2048]{2,1,0:T(8,128)(2,1)} %copy-done.2, bf16[2048,5,128]{0,2,1:T(8,128)(2,1)} %bitcast.105), kind=kOutput, calls=%fused_computation.31 | convolution fusion | flops 671416320 | bytes 8192000 | tf_op jit(solution)/shard_map/while/body/eval_jaxpr/hrk,khs->rhs/dot_general | solution.py:55
  236.0 0.9 copy.145
  236.9 129.5 %psum.7 = f32[2,5]{1,0:T(2,128)S(1)} all-reduce(f32[2,5]{1,0:T(2,128)S(1)} %maximum_negate_fusion), channel_id=1, replica_groups=mesh['seq'=16,'head'=4,'dp'=4] {'seq','dp'}, use_global_device_ids=true, to_apply=%region_10.11 | all-reduce | flops 10 | bytes 80 | tf_op jit(solution)/shard_map/psum | solution.py:160
  366.3 2.6 fusion.21
  369.0 0.9 convert_element_type.95
  369.9 4.8 %all-to-all-start.4 = ((bf16[4,32,640]{2,1,0:T(8,128)(2,1)}), bf16[4,32,640]{2,1,0:T(8,128)(2,1)S(1)}, u32[]{:S(2)}, u32[]{:S(2)}) async-start(bf16[4,32,640]{2,1,0:T(8,128)(2,1)} %convert_element_type.95), calls=%async_computation.4 | async-start | bytes 327680 | tf_op jit(solution)/shard_map/all_to_all | solution.py:146
  374.7 1.1 convert.8
  375.8 0.8 fusion.27
  376.6 2.8 all-to-all-done.4
  379.4 4.8 %all-to-all-start.5 = ((bf16[4,32,640]{2,1,0:T(8,128)(2,1)}), bf16[4,32,640]{2,1,0:T(8,128)(2,1)S(1)}, u32[]{:S(2)}, u32[]{:S(2)}) async-start(bf16[4,32,640]{2,1,0:T(8,128)(2,1)} %bitcast.21), calls=%async_computation.6 | async-start | bytes 327680 | tf_op jit(solution)/shard_map/all_to_all | solution.py:153
  384.2 0.6 broadcast_multiply_fusion
  384.8 0.7 broadcast_in_dim.107
  385.6 1.1 convert.9
  386.7 2.2 all-to-all-done.5
  388.9 4.8 %all-to-all-start.6 = ((bf16[4,32,640]{2,1,0:T(8,128)(2,1)}), bf16[4,32,640]{2,1,0:T(8,128)(2,1)S(1)}, u32[]{:S(2)}, u32[]{:S(2)}) async-start(bf16[4,32,640]{2,1,0:T(8,128)(2,1)} %bitcast.23), calls=%async_computation.7 | async-start | bytes 327680 | tf_op jit(solution)/shard_map/all_to_all | solution.py:156
  393.7 0.7 slice_bitcast_fusion
  394.5 0.7 broadcast_in_dim.108
  395.2 3.1 all-to-all-done.6
  398.4 0.7 broadcast_in_dim.109
  (61 shorter events, 3.1 us)
Async XLA Ops:
  7.2 143.6 %copy-start = (s32[1,4096]{1,0:T(1,128)S(1)}, s32[1,4096]{1,0:T(1,128)}, u32[]{:S(2)}) copy-start(s32[1,4096]{1,0:T(1,128)} %param.23) | copy-start | bytes 49156
  7.2 36.3 %copy-start.9 = (bf16[1,32,2560]{2,1,0:T(8,128)(2,1)S(1)}, bf16[1,32,2560]{2,1,0:T(8,128)(2,1)}, u32[]{:S(2)}) copy-start(bf16[1,32,2560]{2,1,0:T(8,128)(2,1)} %param.15) | copy-start | bytes 491524
  7.2 41.8 %copy-start.10 = (f32[2,5]{1,0:T(2,128)S(1)}, f32[2,5]{1,0:T(2,128)}, u32[]{:S(2)}) copy-start(f32[2,5]{1,0:T(2,128)} %param.20) | copy-start | bytes 124
  7.2 53.1 %all-gather.7.cloned.1.call-start = ((), (), s32[]{:S(2)}) async-start(), calls=%async_computation.9 | async-start | bytes 2785280 | tf_op jit(solution)/shard_map/all_gather | solution.py:104
  18.3 82.7 %all-gather.9.cloned.1.call-start = ((), (), s32[]{:S(2)}) async-start(), calls=%async_computation.10 | async-start | bytes 2785280 | tf_op jit(solution)/shard_map/all_gather | solution.py:105
  28.6 123.8 %all-gather.11.cloned.1.call-start = ((), (), s32[]{:S(2)}) async-start(), calls=%async_computation.13 | async-start | bytes 2785280 | tf_op jit(solution)/shard_map/all_gather | solution.py:162
  32.1 12.1 %all-to-all-start = ((bf16[32,4,640]{2,0,1:T(8,128)(2,1)}), bf16[32,4,640]{2,0,1:T(8,128)(2,1)S(1)}, u32[]{:S(2)}, u32[]{:S(2)}) async-start(bf16[32,4,640]{2,0,1:T(8,128)(2,1)} %copy.116), calls=%async_computation | async-start | bytes 327680 | tf_op jit(solution)/shard_map/all_to_all | solution.py:96
  36.8 152.2 %all-gather.13.cloned.1.call-start = ((), (), s32[]{:S(2)}) async-start(), calls=%async_computation.14 | async-start | bytes 2785280 | tf_op jit(solution)/shard_map/all_gather | solution.py:163
  44.2 9.5 %all-to-all-start.2 = ((bf16[32,4,640]{2,0,1:T(8,128)(2,1)}), bf16[32,4,640]{2,0,1:T(8,128)(2,1)S(1)}, u32[]{:S(2)}, u32[]{:S(2)}) async-start(bf16[32,4,640]{2,0,1:T(8,128)(2,1)} %copy.121), calls=%async_computation.2 | async-start | bytes 327680 | tf_op jit(solution)/shard_map/all_to_all | solution.py:99
  49.0 325.7 %reduce-scatter.3.cloned.1.call-start = ((), (), s32[]{:S(2)}) async-start(), calls=%async_computation.11 | async-start | bytes 11141120 | tf_op jit(solution)/shard_map/reduce_scatter | solution.py:131
  63.3 45.8 %copy-start.3 = (bf16[2048,640]{0,1:T(8,128)(2,1)}, bf16[2048,640]{0,1:T(8,128)(2,1)S(1)}, u32[]{:S(2)}) copy-start(bf16[2048,640]{0,1:T(8,128)(2,1)S(1)} %copy.118) | copy-start | bytes 7864324
  109.1 2.7 copy-start.4
  109.1 3.6 copy-start.7
  112.7 1.3 copy-start.5
  112.7 1.6 copy-start.6
  148.4 1.0 copy-start.8
  148.5 237.1 %reduce-scatter.5.cloned.1.call-start = ((), (), s32[]{:S(2)}) async-start(), calls=%async_computation.12 | async-start | bytes 11141120 | tf_op jit(solution)/shard_map/reduce_scatter | solution.py:193
  189.0 6.1 %slice-start = ((s8[10485760]{0:T(1024)(128)(4,1)}), s8[4194304]{0:T(1024)(128)(4,1)S(1)}, s32[]{:S(2)}) async-start(s8[10485760]{0:T(1024)(128)(4,1)} %bitcast.80), calls=%async_computation.15 | async-start | bytes 8388608
  189.0 7.3 %slice-start.1 = ((s8[10485760]{0:T(1024)(128)(4,1)}), s8[4194304]{0:T(1024)(128)(4,1)S(1)}, s32[]{:S(2)}) async-start(s8[10485760]{0:T(1024)(128)(4,1)} %bitcast.80), calls=%async_computation.16 | async-start | bytes 8388608
  189.0 7.9 %slice-start.2 = ((s8[10485760]{0:T(1024)(128)(4,1)}), s8[2097152]{0:T(1024)(128)(4,1)S(1)}, s32[]{:S(2)}) async-start(s8[10485760]{0:T(1024)(128)(4,1)} %bitcast.80), calls=%async_computation.17 | async-start | bytes 4194304
  198.6 4.0 copy-start.2
  236.9 162.3 %copy-start.1 = (s32[1,4096]{1,0:T(1,128)S(1)}, s32[1,4096]{1,0:T(1,128)}, u32[]{:S(2)}) copy-start(s32[1,4096]{1,0:T(1,128)} %param.23) | copy-start | bytes 49156
  369.9 9.5 %all-to-all-start.4 = ((bf16[4,32,640]{2,1,0:T(8,128)(2,1)}), bf16[4,32,640]{2,1,0:T(8,128)(2,1)S(1)}, u32[]{:S(2)}, u32[]{:S(2)}) async-start(bf16[4,32,640]{2,1,0:T(8,128)(2,1)} %convert_element_type.95), calls=%async_computation.4 | async-start | bytes 327680 | tf_op jit(solution)/shard_map/all_to_all | solution.py:146
  379.4 9.5 %all-to-all-start.5 = ((bf16[4,32,640]{2,1,0:T(8,128)(2,1)}), bf16[4,32,640]{2,1,0:T(8,128)(2,1)S(1)}, u32[]{:S(2)}, u32[]{:S(2)}) async-start(bf16[4,32,640]{2,1,0:T(8,128)(2,1)} %bitcast.21), calls=%async_computation.6 | async-start | bytes 327680 | tf_op jit(solution)/shard_map/all_to_all | solution.py:153
  388.9 9.5 %all-to-all-start.6 = ((bf16[4,32,640]{2,1,0:T(8,128)(2,1)}), bf16[4,32,640]{2,1,0:T(8,128)(2,1)S(1)}, u32[]{:S(2)}, u32[]{:S(2)}) async-start(bf16[4,32,640]{2,1,0:T(8,128)(2,1)} %bitcast.23), calls=%async_computation.7 | async-start | bytes 327680 | tf_op jit(solution)/shard_map/all_to_all | solution.py:156
Sparse Core Ops, SparseCore 0:
  18.5 41.7 all-gather.6
  62.1 38.8 all-gather.8
  103.4 41.4 all-gather.10
  147.0 41.9 all-gather.12
  191.4 73.8 reduce-scatter.2
  267.7 74.0 reduce-scatter.4
where the time goes:
time: 408 us; the launch traced here: 406 us
  blocking collectives  149 us (37%)
  waiting for transfers between devices  83.5 us (20%)
  local copies, waits for them, and re-layouts  52.1 us (13%)
  matrix products  50.7 us (12%)
  other arithmetic  32.3 us (8%)
  starting transfers between devices  24.2 us (6%)
  between operations  14.4 us (4%)
    psum x1, blocking collectives, local(): slope_grad = lax.psum(slope_local, ('seq', 'dp')) / patch_total  129 us
    all_gather x1, waiting for transfers between devices, local(): lax.all_gather(local_values, 'seq', axis=0, tiled=True)  37.8 us
    all_gather x1, waiting for transfers between devices, local(): lax.all_gather(memory_values[0], 'seq', axis=0, tiled=True)  27.1 us
    another operation x4, local copies, waits for them, and re-layouts, key_terms(): jnp.stack([key_grad.reshape(row_count, -1), value_grad.reshape(row_count,...  23.7 us
    another operation x2, other arithmetic, key_terms(): jnp.stack([key_grad.reshape(row_count, -1), value_grad.reshape(row_count,...  17.5 us
    dot_general x2, matrix products, key_terms(): jnp.einsum('chrk,crhs->khs', softmax_b, grad_rows, preferred_element_type...  15.4 us
    unnamed x33, local copies, waits for them, and re-layouts  10.6 us
    all_to_all x1, blocking collectives, local(): lax.all_to_all(self_keys[0], 'head', split_axis=1, concat_axis=0, tiled=T...  10 us
  transfers between devices with their start and end apart: 11, of which 7 were waited for; matrix products, arithmetic and copies ran while one was open for 31% of the time, Pallas kernels for 0%

commit v1 on v0

--- a/solution.py
+++ b/solution.py
@@ -160,7 +160,10 @@
     slope_grad = lax.psum(slope_local, ("seq", "dp")) / patch_total
     memory_all_keys, memory_all_values = (
         lax.all_gather(memory_keys[0], "seq", axis=0, tiled=True),
-        lax.all_gather(memory_values[0], "seq", axis=0, tiled=True),
+        jnp.concatenate(
+            lax.all_to_all(jnp.stack([memory_values[0]] * lax.axis_size("seq")), "seq", 0, 0),
+            axis=0,
+        ),
     )
     memory_all_key_heads = heads_of(memory_all_keys, head_count)
     memory_all_value_heads = heads_of(memory_all_values, head_count)

time: 408 us -> 466 us (1.14)
  waiting for transfers between devices: 83.5 us -> 127 us
  local copies, waits for them, and re-layouts: 52.1 us -> 63 us
    all_to_all x0 -> x1, waiting for transfers between devices: none -> 69.1 us  [local(): lax.all_to_all(jnp.stack([memory_values[0]] * lax.axis_size('seq')), 'seq...]
    all_gather x1 -> x0, waiting for transfers between devices: 27.1 us -> none  [local(): lax.all_gather(memory_values[0], 'seq', axis=0, tiled=True)]
    another operation x0 -> x3, local copies, waits for them, and re-layouts: none -> 7.37 us  [the longest x1 5.23 us: heads_of(): return matrix.reshape(matrix.shape[0], head_count, -1)]
    all_to_all x0 -> x1, local copies, waits for them, and re-layouts: none -> 4.93 us  [local(): lax.all_to_all(jnp.stack([memory_values[0]] * lax.axis_size('seq')), 'seq...]
    unnamed x33 -> x34, local copies, waits for them, and re-layouts: 10.6 us -> 9.19 us
  transfers between devices with their start and end apart: 11 -> 11, of which waited for: 7 -> 7; matrix products, arithmetic and copies ran while one was open for 31% -> 30% of each run, Pallas kernels for 0% -> 0%
where the time goes in v1:
time: 466 us; the launch traced here: 464 us
  blocking collectives  148 us (32%)
  waiting for transfers between devices  127 us (27%)
  local copies, waits for them, and re-layouts  63 us (14%)
  matrix products  50.8 us (11%)
  other arithmetic  32.2 us (7%)
  starting transfers between devices  28.7 us (6%)
  between operations  14.1 us (3%)
    psum x1, blocking collectives, local(): slope_grad = lax.psum(slope_local, ('seq', 'dp')) / patch_total  129 us
    all_to_all x1, waiting for transfers between devices, local(): lax.all_to_all(jnp.stack([memory_values[0]] * lax.axis_size('seq')), 'seq...  69.1 us
    all_gather x1, waiting for transfers between devices, local(): lax.all_gather(local_values, 'seq', axis=0, tiled=True)  37.8 us
    another operation x4, local copies, waits for them, and re-layouts, key_terms(): jnp.stack([key_grad.reshape(row_count, -1), value_grad.reshape(row_count,...  23.7 us
    another operation x2, other arithmetic, key_terms(): jnp.stack([key_grad.reshape(row_count, -1), value_grad.reshape(row_count,...  17.4 us
    dot_general x2, matrix products, key_terms(): jnp.einsum('chrk,crhs->khs', softmax_b, grad_rows, preferred_element_type...  15.3 us
    all_to_all x1, blocking collectives, local(): lax.all_to_all(self_keys[0], 'head', split_axis=1, concat_axis=0, tiled=T...  10 us
    sub x1, matrix products, query_side(): weights = jnp.exp(scores - row_max)  9.55 us
  transfers between devices with their start and end apart: 11, of which 7 were waited for; matrix products, arithmetic and copies ran while one was open for 30% of the time, Pallas kernels for 0%

profile of v1, /device:TPU:2, one launch (start us, length us, event | category | flops | bytes accessed | tf_op | source)
XLA Modules:
  0.0 463.9 jit_solution(15283107263724420395)
XLA Ops:
  7.3 1.0 all_to_all.88
  8.3 10.0 %all_to_all.114 = bf16[32,4,640]{2,0,1:T(8,128)(2,1)} all-to-all(bf16[32,4,640]{2,0,1:T(8,128)(2,1)S(1)} %copy.118), channel_id=1, replica_groups=mesh['seq'=16,'head'=4,'dp'=4] {'head'}, dimensions={1} | all-to-all | bytes 327680 | tf_op jit(solution)/shard_map/all_to_all | solution.py:97
  18.4 1.0 all_to_all.95
  19.4 9.2 %all_to_all.115 = bf16[32,4,640]{2,0,1:T(8,128)(2,1)} all-to-all(bf16[32,4,640]{2,0,1:T(8,128)(2,1)S(1)} %copy.123), channel_id=1, replica_groups=mesh['seq'=16,'head'=4,'dp'=4] {'head'}, dimensions={1} | all-to-all | bytes 327680 | tf_op jit(solution)/shard_map/all_to_all | solution.py:98
  28.6 1.0 all_to_all.85
  29.6 0.7 copy.117
  30.3 4.8 %all-to-all-start = ((bf16[32,4,640]{2,0,1:T(8,128)(2,1)}), bf16[32,4,640]{2,0,1:T(8,128)(2,1)S(1)}, u32[]{:S(2)}, u32[]{:S(2)}) async-start(bf16[32,4,640]{2,0,1:T(8,128)(2,1)} %copy.117), calls=%async_computation | async-start | bytes 327680 | tf_op jit(solution)/shard_map/all_to_all | solution.py:96
  35.0 1.7 copy.137
  36.8 0.8 reduce-window.4
  38.5 0.8 select_reduce_fusion.1
  39.6 1.8 abs_convert_fusion
  41.7 0.7 copy.122
  42.4 4.8 %all-to-all-start.2 = ((bf16[32,4,640]{2,0,1:T(8,128)(2,1)}), bf16[32,4,640]{2,0,1:T(8,128)(2,1)S(1)}, u32[]{:S(2)}, u32[]{:S(2)}) async-start(bf16[32,4,640]{2,0,1:T(8,128)(2,1)} %copy.122), calls=%async_computation.2 | async-start | bytes 327680 | tf_op jit(solution)/shard_map/all_to_all | solution.py:99
  47.6 4.3 all-to-all-done.2
  52.3 7.9 %all-gather.5.cloned.1.call-done = bf16[2048,640]{1,0:T(8,128)(2,1)} async-done(((bf16[128,640]{1,0:T(8,128)(2,1)}), bf16[2048,640]{1,0:T(8,128)(2,1)}) %all-gather.5.cloned.1.call-update) | async-done | bytes 2621456 | tf_op jit(solution)/shard_map/all_gather | solution.py:104
  60.3 3.0 copy.119
  63.3 37.8 %all-gather.7.cloned.1.call-done = bf16[2048,640]{1,0:T(8,128)(2,1)} async-done(((bf16[128,640]{1,0:T(8,128)(2,1)}), bf16[2048,640]{1,0:T(8,128)(2,1)}) %all-gather.7.cloned.1.call-update) | async-done | bytes 2621456 | tf_op jit(solution)/shard_map/all_gather | solution.py:105
  101.0 4.5 copy.124
  105.5 3.6 select_add_fusion
  109.1 1.6 fusion.28
  110.7 1.0 copy-done.4
  111.7 1.0 copy-done.7
  112.7 1.3 multiply_reduce_fusion.3
  114.3 2.4 multiply_reduce_fusion.2
  116.7 3.2 convolution_multiply_fusion
  119.8 6.0 %copy.132 = f32[2048,1,640]{2,0,1:T(8,128)} copy(f32[2048,1,640]{0,2,1:T(8,128)} %bitcast.81) | data formatting | bytes 10485760 | tf_op jit(solution)/shard_map/stack;reshape | solution.py:77
  125.8 8.0 %fusion.7 = f32[5,2048,128]{1,2,0:T(8,128)} fusion(bf16[128,5,128]{0,2,1:T(8,128)(2,1)S(1)} %copy.131, f32[5,128]{1,0:T(8,128)S(1)} %get-tuple-element.85, f32[5,128,2048]{2,1,0:T(8,128)} %copy-done.4), kind=kOutput, calls=%fused_computation.22 | convolution fusion | flops 339479168 | bytes 10652160 | tf_op jit(solution)/shard_map/chrk,crhs->khs/dot_general | solution.py:74
  133.7 5.9 %copy.133 = f32[2048,1,640]{2,0,1:T(8,128)} copy(f32[2048,1,640]{0,2,1:T(8,128)} %bitcast.86) | data formatting | bytes 10485760 | tf_op jit(solution)/shard_map/stack;reshape | solution.py:77
  139.6 8.8 %pad_maximum_fusion = f32[2048,2,640]{2,0,1:T(8,128)} fusion(f32[2048,1,640]{2,0,1:T(8,128)} %copy.133, f32[2048,1,640]{2,0,1:T(8,128)} %copy.132), kind=kLoop, calls=%fused_computation.2 | loop fusion | flops 2621440 | bytes 20971520 | tf_op jit(solution)/shard_map/stack | solution.py:77
  148.5 0.9 copy-done.10
  149.5 2.0 stack.22
  151.5 4.7 %all-to-all-start.7 = ((bf16[16,128,640]{1,2,0:T(8,128)(2,1)}), bf16[16,128,640]{1,2,0:T(8,128)(2,1)}, u32[]{:S(2)}, u32[]{:S(2)}) async-start(bf16[16,128,640]{1,2,0:T(8,128)(2,1)} %stack.22), calls=%async_computation.8 | async-start | bytes 5242880 | tf_op jit(solution)/shard_map/all_to_all | solution.py:164
  156.4 1.1 copy.140
  157.6 1.6 compare_select_fusion
  159.2 69.1 %all-to-all-done.7 = bf16[16,128,640]{1,2,0:T(8,128)(2,1)} async-done(((bf16[16,128,640]{1,2,0:T(8,128)(2,1)}), bf16[16,128,640]{1,2,0:T(8,128)(2,1)}, u32[]{:S(2)}, u32[]{:S(2)}) %all-to-all-start.7) | async-done | bytes 2621472 | tf_op jit(solution)/shard_map/all_to_all | solution.py:164
  228.3 4.9 %copy.142 = bf16[16,128,640]{1,0,2:T(8,128)(2,1)} copy(bf16[16,128,640]{1,2,0:T(8,128)(2,1)} %all-to-all-done.7) | data formatting | bytes 5242880 | tf_op jit(solution)/shard_map/all_to_all | solution.py:164
  233.2 5.2 %reshape_reshape.3 = bf16[2048,5,128]{0,2,1:T(8,128)(2,1)} reshape(bf16[16,128,640]{1,0,2:T(8,128)(2,1)} %copy.142) | data formatting | bytes 5242880 | tf_op jit(solution)/shard_map/reshape;reshape | solution.py:26
  238.4 9.5 %fusion.29 = (f32[5,256]{1,0:T(8,128)S(1)}, f32[5,256,2048]{2,1,0:T(8,128)}) fusion(f32[256,2048]{1,0:T(8,128)} %compare_select_fusion, bf16[256,5,128]{0,2,1:T(8,128)(2,1)S(1)} %bitcast.89, bf16[2048,5,128]{0,2,1:T(8,128)(2,1)} %bitcast.107), kind=kOutput, calls=%fused_computation.62 | convolution fusion | flops 681576448 | bytes 15537152 | tf_op jit(solution)/shard_map/while/body/eval_jaxpr/sub | solution.py:44
  248.0 6.3 %multiply_reduce_fusion = (f32[5,256]{1,0:T(8,128)S(1)}, f32[5,256,2048]{2,1,0:T(8,128)S(1)}) fusion(f32[5,256,2048]{2,1,0:T(8,128)} %get-tuple-element.90, f32[5,256]{1,0:T(8,128)S(1)} %get-tuple-element.89, bf16[256,5,128]{0,2,1:T(8,128)(2,1)S(1)} %bitcast.98, bf16[2048,5,128]{0,2,1:T(8,128)(2,1)} %reshape_reshape.3), kind=kOutput, calls=%fused_computation.5 | convolution fusion | flops 678951680 | bytes 23930880 | tf_op jit(solution)/shard_map/while/body/eval_jaxpr/rhs,khs->hrk/dot_general | solution.py:48
  254.3 1.3 slice-done.1
  256.2 1.8 multiply_convert_fusion
  258.0 3.9 convolution_multiply_fusion.1
  262.0 5.9 %copy.145 = f32[2048,1,640]{2,0,1:T(8,128)} copy(f32[2048,1,640]{0,2,1:T(8,128)} %bitcast.80) | data formatting | bytes 10485760 | tf_op jit(solution)/shard_map/stack;reshape | solution.py:77
  268.0 7.4 %fusion.3 = f32[5,2048,128]{1,2,0:T(8,128)} fusion(bf16[256,5,128]{0,2,1:T(8,128)(2,1)S(1)} %bitcast.99, f32[5,256,2048]{2,1,0:T(8,128)} %get-tuple-element.90, f32[5,256]{1,0:T(8,128)S(1)} %get-tuple-element.89), kind=kOutput, calls=%fused_computation.9 | convolution fusion | flops 676331520 | bytes 16061440 | tf_op jit(solution)/shard_map/chrk,crhs->khs/dot_general | solution.py:74
  275.3 5.9 %copy.146 = f32[2048,1,640]{2,0,1:T(8,128)} copy(f32[2048,1,640]{0,2,1:T(8,128)} %bitcast.87) | data formatting | bytes 10485760 | tf_op jit(solution)/shard_map/stack;reshape | solution.py:77
  281.2 8.6 %pad_maximum_fusion.1 = f32[2048,2,640]{2,0,1:T(8,128)} fusion(f32[2048,1,640]{2,0,1:T(8,128)} %copy.146, f32[2048,1,640]{2,0,1:T(8,128)} %copy.145), kind=kLoop, calls=%fused_computation.3 | loop fusion | flops 2621440 | bytes 20971520 | tf_op jit(solution)/shard_map/stack | solution.py:77
  289.8 5.2 %fusion.14 = bf16[5,256,128]{1,2,0:T(8,128)(2,1)S(1)} fusion(bf16[5,256,2048]{2,1,0:T(8,128)(2,1)} %copy-done.2, bf16[2048,5,128]{0,2,1:T(8,128)(2,1)} %bitcast.108), kind=kOutput, calls=%fused_computation.31 | convolution fusion | flops 671416320 | bytes 8192000 | tf_op jit(solution)/shard_map/while/body/eval_jaxpr/hrk,khs->rhs/dot_general | solution.py:55
  295.0 0.9 copy.147
  295.9 128.6 %psum.7 = f32[2,5]{1,0:T(2,128)S(1)} all-reduce(f32[2,5]{1,0:T(2,128)S(1)} %maximum_negate_fusion), channel_id=1, replica_groups=mesh['seq'=16,'head'=4,'dp'=4] {'seq','dp'}, use_global_device_ids=true, to_apply=%region_10.11 | all-reduce | flops 10 | bytes 80 | tf_op jit(solution)/shard_map/psum | solution.py:160
  424.5 2.6 fusion.21
  427.3 0.9 convert_element_type.95
  428.1 4.8 %all-to-all-start.4 = ((bf16[4,32,640]{2,1,0:T(8,128)(2,1)}), bf16[4,32,640]{2,1,0:T(8,128)(2,1)S(1)}, u32[]{:S(2)}, u32[]{:S(2)}) async-start(bf16[4,32,640]{2,1,0:T(8,128)(2,1)} %convert_element_type.95), calls=%async_computation.4 | async-start | bytes 327680 | tf_op jit(solution)/shard_map/all_to_all | solution.py:146
  432.9 1.1 convert.8
  434.1 0.8 fusion.27
  434.8 2.8 all-to-all-done.4
  437.6 4.8 %all-to-all-start.5 = ((bf16[4,32,640]{2,1,0:T(8,128)(2,1)}), bf16[4,32,640]{2,1,0:T(8,128)(2,1)S(1)}, u32[]{:S(2)}, u32[]{:S(2)}) async-start(bf16[4,32,640]{2,1,0:T(8,128)(2,1)} %bitcast.21), calls=%async_computation.6 | async-start | bytes 327680 | tf_op jit(solution)/shard_map/all_to_all | solution.py:153
  443.1 0.7 broadcast_in_dim.107
  443.8 1.1 convert.9
  444.9 2.2 all-to-all-done.5
  447.1 4.8 %all-to-all-start.6 = ((bf16[4,32,640]{2,1,0:T(8,128)(2,1)}), bf16[4,32,640]{2,1,0:T(8,128)(2,1)S(1)}, u32[]{:S(2)}, u32[]{:S(2)}) async-start(bf16[4,32,640]{2,1,0:T(8,128)(2,1)} %bitcast.23), calls=%async_computation.7 | async-start | bytes 327680 | tf_op jit(solution)/shard_map/all_to_all | solution.py:156
  451.9 0.7 slice_bitcast_fusion
  452.7 0.7 broadcast_in_dim.108
  453.4 3.1 all-to-all-done.6
  456.7 0.7 broadcast_in_dim.109
  (65 shorter events, 4.9 us)
Async XLA Ops:
  7.2 150.4 %copy-start = (s32[1,4096]{1,0:T(1,128)S(1)}, s32[1,4096]{1,0:T(1,128)}, u32[]{:S(2)}) copy-start(s32[1,4096]{1,0:T(1,128)} %param.23) | copy-start | bytes 49156
  7.2 34.5 %copy-start.9 = (bf16[1,32,2560]{2,1,0:T(8,128)(2,1)S(1)}, bf16[1,32,2560]{2,1,0:T(8,128)(2,1)}, u32[]{:S(2)}) copy-start(bf16[1,32,2560]{2,1,0:T(8,128)(2,1)} %param.15) | copy-start | bytes 491524
  7.2 40.0 %copy-start.11 = (f32[2,5]{1,0:T(2,128)S(1)}, f32[2,5]{1,0:T(2,128)}, u32[]{:S(2)}) copy-start(f32[2,5]{1,0:T(2,128)} %param.20) | copy-start | bytes 124
  7.2 53.1 %all-gather.5.cloned.1.call-start = ((), (), s32[]{:S(2)}) async-start(), calls=%async_computation.10 | async-start | bytes 2785280 | tf_op jit(solution)/shard_map/all_gather | solution.py:104
  18.3 82.7 %all-gather.7.cloned.1.call-start = ((), (), s32[]{:S(2)}) async-start(), calls=%async_computation.11 | async-start | bytes 2785280 | tf_op jit(solution)/shard_map/all_gather | solution.py:105
  30.3 12.1 %all-to-all-start = ((bf16[32,4,640]{2,0,1:T(8,128)(2,1)}), bf16[32,4,640]{2,0,1:T(8,128)(2,1)S(1)}, u32[]{:S(2)}, u32[]{:S(2)}) async-start(bf16[32,4,640]{2,0,1:T(8,128)(2,1)} %copy.117), calls=%async_computation | async-start | bytes 327680 | tf_op jit(solution)/shard_map/all_to_all | solution.py:96
  35.0 203.4 %all-gather.9.cloned.1.call-start = ((), (), s32[]{:S(2)}) async-start(), calls=%async_computation.14 | async-start | bytes 2785280 | tf_op jit(solution)/shard_map/all_gather | solution.py:162
  42.4 9.5 %all-to-all-start.2 = ((bf16[32,4,640]{2,0,1:T(8,128)(2,1)}), bf16[32,4,640]{2,0,1:T(8,128)(2,1)S(1)}, u32[]{:S(2)}, u32[]{:S(2)}) async-start(bf16[32,4,640]{2,0,1:T(8,128)(2,1)} %copy.122), calls=%async_computation.2 | async-start | bytes 327680 | tf_op jit(solution)/shard_map/all_to_all | solution.py:99
  47.2 385.7 %reduce-scatter.3.cloned.1.call-start = ((), (), s32[]{:S(2)}) async-start(), calls=%async_computation.12 | async-start | bytes 11141120 | tf_op jit(solution)/shard_map/reduce_scatter | solution.py:131
  63.3 45.8 %copy-start.3 = (bf16[2048,640]{0,1:T(8,128)(2,1)}, bf16[2048,640]{0,1:T(8,128)(2,1)S(1)}, u32[]{:S(2)}) copy-start(bf16[2048,640]{0,1:T(8,128)(2,1)S(1)} %copy.119) | copy-start | bytes 7864324
  109.1 2.7 copy-start.4
  109.1 3.6 copy-start.7
  112.7 1.3 copy-start.5
  112.7 1.6 copy-start.6
  148.4 0.9 copy-start.10
  148.5 7.7 %copy-start.8 = (bf16[1,256,640]{2,1,0:T(8,128)(2,1)S(1)}, bf16[1,256,640]{2,1,0:T(8,128)(2,1)}, u32[]{:S(2)}) copy-start(bf16[1,256,640]{2,1,0:T(8,128)(2,1)} %param.16) | copy-start | bytes 983044
  151.5 76.8 %all-to-all-start.7 = ((bf16[16,128,640]{1,2,0:T(8,128)(2,1)}), bf16[16,128,640]{1,2,0:T(8,128)(2,1)}, u32[]{:S(2)}, u32[]{:S(2)}) async-start(bf16[16,128,640]{1,2,0:T(8,128)(2,1)} %stack.22), calls=%async_computation.8 | async-start | bytes 5242880 | tf_op jit(solution)/shard_map/all_to_all | solution.py:164
  156.2 287.6 %reduce-scatter.5.cloned.1.call-start = ((), (), s32[]{:S(2)}) async-start(), calls=%async_computation.13 | async-start | bytes 11141120 | tf_op jit(solution)/shard_map/reduce_scatter | solution.py:196
  248.0 6.3 %slice-start = ((s8[10485760]{0:T(1024)(128)(4,1)}), s8[4194304]{0:T(1024)(128)(4,1)S(1)}, s32[]{:S(2)}) async-start(s8[10485760]{0:T(1024)(128)(4,1)} %bitcast.82), calls=%async_computation.15 | async-start | bytes 8388608
  248.0 7.6 %slice-start.1 = ((s8[10485760]{0:T(1024)(128)(4,1)}), s8[4194304]{0:T(1024)(128)(4,1)S(1)}, s32[]{:S(2)}) async-start(s8[10485760]{0:T(1024)(128)(4,1)} %bitcast.82), calls=%async_computation.16 | async-start | bytes 8388608
  248.0 8.3 %slice-start.2 = ((s8[10485760]{0:T(1024)(128)(4,1)}), s8[2097152]{0:T(1024)(128)(4,1)S(1)}, s32[]{:S(2)}) async-start(s8[10485760]{0:T(1024)(128)(4,1)} %bitcast.82), calls=%async_computation.17 | async-start | bytes 4194304
  258.0 4.0 copy-start.2
  295.9 161.5 %copy-start.1 = (s32[1,4096]{1,0:T(1,128)S(1)}, s32[1,4096]{1,0:T(1,128)}, u32[]{:S(2)}) copy-start(s32[1,4096]{1,0:T(1,128)} %param.23) | copy-start | bytes 49156
  428.1 9.5 %all-to-all-start.4 = ((bf16[4,32,640]{2,1,0:T(8,128)(2,1)}), bf16[4,32,640]{2,1,0:T(8,128)(2,1)S(1)}, u32[]{:S(2)}, u32[]{:S(2)}) async-start(bf16[4,32,640]{2,1,0:T(8,128)(2,1)} %convert_element_type.95), calls=%async_computation.4 | async-start | bytes 327680 | tf_op jit(solution)/shard_map/all_to_all | solution.py:146
  437.6 9.5 %all-to-all-start.5 = ((bf16[4,32,640]{2,1,0:T(8,128)(2,1)}), bf16[4,32,640]{2,1,0:T(8,128)(2,1)S(1)}, u32[]{:S(2)}, u32[]{:S(2)}) async-start(bf16[4,32,640]{2,1,0:T(8,128)(2,1)} %bitcast.21), calls=%async_computation.6 | async-start | bytes 327680 | tf_op jit(solution)/shard_map/all_to_all | solution.py:153
  447.1 9.5 %all-to-all-start.6 = ((bf16[4,32,640]{2,1,0:T(8,128)(2,1)}), bf16[4,32,640]{2,1,0:T(8,128)(2,1)S(1)}, u32[]{:S(2)}, u32[]{:S(2)}) async-start(bf16[4,32,640]{2,1,0:T(8,128)(2,1)} %bitcast.23), calls=%async_computation.7 | async-start | bytes 327680 | tf_op jit(solution)/shard_map/all_to_all | solution.py:156
Sparse Core Ops, SparseCore 0:
  18.5 41.7 all-gather.4
  62.1 38.8 all-gather.6
  103.4 41.4 all-gather.8
  148.6 126.5 reduce-scatter.2
  289.9 75.9 reduce-scatter.4
